TPU v7x, 256 devices: a whole 4x4x8 slice. The times are simulated.
256 devices in a mesh: dp: 32 (over y, z_lo, core), tensor: 8 (over x, z_hi).
Axes of the slice: x: 4, y: 4, z: 8 (z_hi: 2, z_lo: 4; z = z_hi * 4 + z_lo), core: 2. Of those that a mesh axis runs over, the one named last changes fastest.
Arguments:
- activations: bfloat16 [32768, 8192], P(('dp', 'tensor')), may hold values from -6 to 6
- output_gradient: bfloat16 [32768, 6144], P('dp', 'tensor'), may hold values from -6 to 6
- packed_weight_nibbles: int32 [2048, 6144], P(None, 'tensor'), may hold values from 0 to 65535
- group_scale_table: float32 [64, 6144], P(None, 'tensor'), may hold values from 0.001275776 to 0.005103104
- dense_feature_index: int32 [64], replicated, may hold values from 0 to 8191, as said below
- dense_feature_weight: float32 [64, 6144], P(None, 'tensor'), may hold values from -0.078125 to 0.078125
- adapter_down_weight: bfloat16 [8192, 16], replicated, may hold values from -0.1875 to 0.1875
- adapter_up_weight: bfloat16 [16, 6144], P(None, 'tensor'), may hold values from -0.0390625 to 0.0390625
Outputs:
- layer_input_gradient: bfloat16 [32768, 8192], P(('dp', 'tensor'))
- down_grad: float32 [8192, 16], replicated
- up_weight_gradient: float32 [16, 6144], P(None, 'tensor')
- outlier_grad: float32 [64, 6144], P(None, 'tensor')
Inputs may be any that keep to these rules, and one draw needn't show every extreme that they name: `packed_weight_nibbles`: each word holds four codes of 0 to 15 in its four lowest groups of four bits, the lowest group for the first of its four input features; every such bit pattern may occur. `dense_feature_index`: distinct and increasing, one in each aligned block of 128 input features, the first 0 and the last 8191.
All inputs are finite; a program needn't handle non-finite values.
Results may differ from a plain program's by a relative error of at most 0.017.
Values may be sent and summed in bfloat16 or wider, within the bound.
A program may use at most 192 MiB of HBM per device.

v0:
```python
import jax
import jax.numpy as jnp
from jax import lax
from jax.sharding import PartitionSpec as P

GROUP = 128


ADAPTER_SCALE = 2.0


def unpack(packed_weight_nibbles, group_scale_table):
    packed_rows = packed_weight_nibbles.shape[0]
    columns = packed_weight_nibbles.shape[1]
    total_rows = packed_rows * 4
    blocks = packed_weight_nibbles.reshape(total_rows // GROUP, GROUP // 4, columns)
    shifts = 4 * jnp.arange(4, dtype=jnp.int32)

    def one_group(pair):
        packed, scale_row = pair
        nibbles = jnp.bitwise_and(jnp.right_shift(packed[:, None, :], shifts[None, :, None]), 15)
        values = (nibbles.astype(jnp.float32) - 8.0) * scale_row[None, None, :]
        return values.reshape(GROUP, columns).astype(jnp.bfloat16)

    return lax.map(one_group, (blocks, group_scale_table)).reshape(total_rows, columns)


def contract_trailing(left, right):
    return lax.dot_general(
        left, right, (((1,), (1,)), ((), ())), preferred_element_type=jnp.float32
    )


def contract_leading(left, right):
    return lax.dot_general(
        left, right, (((0,), (0,)), ((), ())), preferred_element_type=jnp.float32
    )


def body(
    activations,
    output_gradient,
    packed_weight_nibbles,
    group_scale_table,
    dense_feature_index,
    dense_feature_weight,
    adapter_down_weight,
    adapter_up_weight,
):
    own_rows = activations.shape[0]
    grad_norm = float(own_rows * lax.axis_size("dp") * lax.axis_size("tensor")) ** (-0.5)
    weight = unpack(packed_weight_nibbles, group_scale_table)
    gradient_rows = output_gradient
    partial_value = contract_trailing(gradient_rows, weight)
    outlier_term = lax.dot_general(
        gradient_rows.astype(jnp.float32),
        dense_feature_weight,
        (((1,), (1,)), ((), ())),
        precision=lax.Precision.HIGHEST,
        preferred_element_type=jnp.float32,
    )
    reduced_sum = lax.psum_scatter(
        partial_value.at[:, dense_feature_index].add(outlier_term).astype(jnp.bfloat16),
        "tensor",
        scatter_dimension=0,
        tiled=True,
    ).astype(jnp.float32)
    rank_partial = contract_trailing(output_gradient, adapter_up_weight)
    rank_gathered = lax.psum(rank_partial, "tensor")
    rank_gradient = (ADAPTER_SCALE * rank_gathered).astype(jnp.bfloat16)
    local_rank_slice = lax.dynamic_slice_in_dim(
        rank_gradient, lax.axis_index("tensor") * own_rows, own_rows, 0
    )
    block_row_span = lax.all_gather(activations, "tensor", axis=0, tiled=True)
    gradient_rows = output_gradient
    hidden_state = jnp.dot(
        block_row_span, adapter_down_weight, preferred_element_type=jnp.float32
    ).astype(jnp.bfloat16)
    up_gradient_total = ADAPTER_SCALE * contract_leading(hidden_state, gradient_rows)
    outlier_total = contract_leading(
        jnp.take(block_row_span, dense_feature_index, axis=1), gradient_rows
    )
    up_weight_gradient, outlier_grad = lax.psum(
        (grad_norm * up_gradient_total, grad_norm * outlier_total), "dp"
    )
    down_grad = lax.psum(
        grad_norm * contract_leading(activations, local_rank_slice), ("dp", "tensor")
    )
    layer_input_gradient = (
        reduced_sum + contract_trailing(local_rank_slice, adapter_down_weight)
    ).astype(jnp.bfloat16)
    return (layer_input_gradient, down_grad, up_weight_gradient, outlier_grad)


def solution(mesh):
    placed = (
        P(("dp", "tensor"), None),
        P("dp", "tensor"),
        P(None, "tensor"),
        P(None, "tensor"),
        P(),
        P(None, "tensor"),
        P(),
        P(None, "tensor"),
    )
    return jax.shard_map(
        body,
        mesh=mesh,
        in_specs=placed,
        out_specs=(P(("dp", "tensor"), None), P(), P(None, "tensor"), P(None, "tensor")),
        check_vma=False,
    )
```

profile of v0, /device:TPU:16, one launch (start us, length us, event | category | flops | bytes accessed | tf_op | source)
XLA Modules:
  0.0 1316.6 jit_solution(1820698158138350135)
XLA Ops:
  7.2 1.3 copy-done
  8.6 1.9 fusion.17
  10.5 4.1 copy.19
  14.7 1.5 fusion.16
  16.3 181.0 %while.13 = (s32[]{:T(128)}, bf16[64,128,768]{2,1,0:T(8,128)(2,1)}, s32[64,32,768]{2,1,0:T(8,128)}, f32[64,768]{1,0:T(8,128)}, s32[]{:T(128)}) while((s32[]{:T(128)}, bf16[64,128,768]{2,1,0:T(8,128)(2,1)}, s32[64,32,768]{2,1,0:T(8,128)}, f32[64,768]{1,0:T(8,128)}, s32[]{:T(128)}) %tuple.49), condition=%wide.region_1.2_spmd.clone, body=%wide.region_0.1_spmd.clone.sunk | while | flops 589830 | bytes 2075761 | solution.py:25
  16.3 0.9 dynamic-slice_bitcast_fusion.2
  24.8 0.9 dynamic-slice_bitcast_fusion.2
  36.1 0.9 dynamic-slice_bitcast_fusion.2
  41.7 0.9 dynamic-slice_bitcast_fusion.2
  44.6 0.9 dynamic-slice_bitcast_fusion.2
  47.4 0.9 dynamic-slice_bitcast_fusion.2
  53.0 0.9 dynamic-slice_bitcast_fusion.2
  58.7 0.9 dynamic-slice_bitcast_fusion.2
  61.5 0.9 dynamic-slice_bitcast_fusion.2
  72.8 0.9 dynamic-slice_bitcast_fusion.2
  75.7 0.9 dynamic-slice_bitcast_fusion.2
  84.2 0.9 dynamic-slice_bitcast_fusion.2
  89.8 0.9 dynamic-slice_bitcast_fusion.2
  92.7 0.9 dynamic-slice_bitcast_fusion.2
  95.5 0.9 dynamic-slice_bitcast_fusion.2
  129.4 0.9 dynamic-slice_bitcast_fusion.2
  132.2 0.9 dynamic-slice_bitcast_fusion.2
  135.1 0.9 dynamic-slice_bitcast_fusion.2
  137.9 0.9 dynamic-slice_bitcast_fusion.2
  143.5 0.9 dynamic-slice_bitcast_fusion.2
  149.2 0.9 dynamic-slice_bitcast_fusion.2
  152.0 0.9 dynamic-slice_bitcast_fusion.2
  157.7 0.9 dynamic-slice_bitcast_fusion.2
  160.5 0.9 dynamic-slice_bitcast_fusion.2
  163.3 0.9 dynamic-slice_bitcast_fusion.2
  185.9 0.9 dynamic-slice_bitcast_fusion.2
  188.8 0.9 dynamic-slice_bitcast_fusion.2
  197.3 21.8 %convolution_bitcast_fusion = f32[1024,8192]{0,1:T(8,128)} fusion(bf16[8192,768]{1,0:T(8,128)(2,1)} %bitcast.24, bf16[1024,768]{1,0:T(8,128)(2,1)S(1)} %copy-done), kind=kOutput, calls=%fused_computation.8 | convolution fusion | flops 12884901888 | bytes 47710208 | tf_op jit(solution)/shard_map/dot_general | solution.py:29
  219.1 23.1 %scatter_fusion = f32[1024,8192]{0,1:T(8,128)} fusion(f32[1024,8192]{0,1:T(8,128)} %convolution_bitcast_fusion, s32[64]{0:T(128)S(1)} %compare_select_fusion, f32[64,1024]{1,0:T(8,128)S(1)} %fusion.16), kind=kCustom, calls=%fused_computation.1 | custom fusion | flops 65536 | bytes 786688 | tf_op jit(solution)/shard_map/scatter-add | solution.py:63
  242.2 17.5 %convert_element_type.43 = bf16[1024,8192]{0,1:T(8,128)(2,1)} convert(f32[1024,8192]{0,1:T(8,128)} %scatter_fusion) | non-fusion elementwise | flops 8388608 | bytes 50331648 | tf_op jit(solution)/shard_map/convert_element_type | solution.py:63
  259.7 20.9 %copy.20 = bf16[1024,8192]{1,0:T(8,128)(2,1)} copy(bf16[1024,8192]{0,1:T(8,128)(2,1)} %convert_element_type.43) | data formatting | bytes 33554432
  280.8 2.8 fusion.4
  283.6 158.8 %all-gather.2.cloned.1.call-done = bf16[1024,8192]{0,1:T(8,128)(2,1)} async-done(((bf16[128,8192]{0,1:T(8,128)(2,1)}), bf16[1024,8192]{0,1:T(8,128)(2,1)}) %all-gather.2.cloned.1.call-update) | async-done | bytes 16777232 | tf_op jit(solution)/shard_map/all_gather | solution.py:74
  442.4 8.4 convolution_multiply_fusion.2
  450.8 153.2 %psum.30 = f32[16,768]{1,0:T(8,128)} all-reduce(f32[16,768]{1,0:T(8,128)S(1)} %convolution_multiply_fusion.2), channel_id=1, replica_groups=mesh['dp'=32,'tensor'=8] {'dp'}, use_global_device_ids=true, to_apply=%region_6.7 | all-reduce | flops 12288 | bytes 98304 | tf_op jit(solution)/shard_map/psum | solution.py:83
  604.0 8.7 gather_fusion
  612.7 1.1 convolution_multiply_fusion.1
  613.9 173.5 %reduce-scatter.4.cloned.1.call-done = bf16[128,8192]{1,0:T(8,128)(2,1)} async-done(((bf16[1024,8192]{1,0:T(8,128)(2,1)}), bf16[128,8192]{1,0:T(8,128)(2,1)}) %reduce-scatter.4.cloned.1.call-update) | async-done | bytes 2097168 | tf_op jit(solution)/shard_map/reduce_scatter | solution.py:62
  787.4 3.7 fusion.3
  791.0 266.1 %all-reduce.6.cloned.1.call-done = f32[8192,16]{0,1:T(8,128)} async-done(((f32[8192,16]{0,1:T(8,128)}), f32[8192,16]{0,1:T(8,128)}) %all-reduce.6.cloned.1.call-update) | async-done | bytes 524304 | tf_op jit(solution)/shard_map/psum | solution.py:86
  1057.1 249.4 %all-reduce.8.cloned.1.call-done = f32[64,768]{1,0:T(8,128)} async-done(((f32[64,768]{1,0:T(8,128)}), f32[64,768]{1,0:T(8,128)}) %all-reduce.8.cloned.1.call-update) | async-done | bytes 196624 | tf_op jit(solution)/shard_map/psum | solution.py:83
  1306.5 1.9 copy.33
  1308.4 1.6 copy.34
  (507 shorter events, 154.9 us)
Async XLA Ops:
  7.2 1.4 copy-start
  7.2 7.5 copy-start.3
  7.2 7.5 copy-start.2
  7.2 273.5 %all-reduce.4.cloned.1.call-start = ((), (), s32[]{:S(2)}) async-start(), calls=%async_computation.1 | async-start | bytes 131072 | tf_op jit(solution)/shard_map/psum | solution.py:69
  10.5 431.9 %all-gather.2.cloned.1.call-start = ((), (), s32[]{:S(2)}) async-start(), calls=%async_computation.3 | async-start | bytes 18874368 | tf_op jit(solution)/shard_map/all_gather | solution.py:74
  14.6 772.7 %reduce-scatter.4.cloned.1.call-start = ((), (), s32[]{:S(2)}) async-start(), calls=%async_computation.5 | async-start | bytes 18874368 | tf_op jit(solution)/shard_map/reduce_scatter | solution.py:62
  280.6 161.8 %copy-start.1 = (bf16[8192,16]{0,1:T(8,128)(2,1)S(1)}, bf16[8192,16]{0,1:T(8,128)(2,1)}, u32[]{:S(2)}) copy-start(bf16[8192,16]{0,1:T(8,128)(2,1)} %param.16) | copy-start | bytes 786436
  280.6 776.5 %all-reduce.6.cloned.1.call-start = ((), (), s32[]{:S(2)}) async-start(), calls=%async_computation.2 | async-start | bytes 1048576 | tf_op jit(solution)/shard_map/psum | solution.py:86
  283.6 1023.0 %all-reduce.8.cloned.1.call-start = ((), (), s32[]{:S(2)}) async-start(), calls=%async_computation.4 | async-start | bytes 393216 | tf_op jit(solution)/shard_map/psum | solution.py:83
Sparse Core Ops, SparseCore 0:
  11.2 107.8 all-reduce.3
  122.5 319.8 all-gather.1
  447.2 340.0 reduce-scatter.3
  794.2 262.9 all-reduce.5
  1060.3 246.1 all-reduce.7
where the time goes:
time: 1340 us; the launch traced here: 1320 us
  waiting for transfers between devices  848 us (63%)
  local copies, waits for them, and re-layouts  165 us (12%)
  blocking collectives  153 us (11%)
  other arithmetic  93.5 us (7%)
  matrix products  41.2 us (3%)
  between operations  13.9 us (1%)
    psum x1, waiting for transfers between devices, body(): lax.psum(grad_norm * contract_leading(activations, local_rank_slice), ('d...  266 us
    psum x1, waiting for transfers between devices, body(): lax.psum((grad_norm * up_gradient_total, grad_norm * outlier_total), 'dp')  249 us
    reduce_scatter x1, waiting for transfers between devices, body(): lax.psum_scatter(partial_value.at[:, dense_feature_index].add(outlier_ter...  174 us
    all_gather x1, waiting for transfers between devices, body(): block_row_span = lax.all_gather(activations, 'tensor', axis=0, tiled=True)  159 us
    psum x1, blocking collectives, body(): lax.psum((grad_norm * up_gradient_total, grad_norm * outlier_total), 'dp')  153 us
    shift_right_arithmetic x320, local copies, waits for them, and re-layouts, one_group(): jnp.right_shift(packed[:, None, :], shifts[None, :, None])  77.4 us
    dynamic_update_slice x64, other arithmetic, unpack(): lax.map(one_group, (blocks, group_scale_table)).reshape(total_rows, columns)  52.7 us
    dynamic_slice x64, local copies, waits for them, and re-layouts, unpack(): lax.map(one_group, (blocks, group_scale_table)).reshape(total_rows, columns)  48.6 us
  transfers between devices with their start and end apart: 5, of which 4 were waited for; matrix products, arithmetic and copies ran while one was open for 22% of the time, Pallas kernels for 0%

commit v1 on v0

v1 whole, which is shorter than its diff:
```python
import functools

import jax
import jax.numpy as jnp
from jax import lax
from jax.experimental import pallas as pl
from jax.experimental.pallas import tpu as pltpu
from jax.sharding import PartitionSpec as P

MESH = pl.DeviceIdType.MESH
F32 = jnp.float32
BF16 = jnp.bfloat16

WIDTH = 8192
FEATS = 768
RANK = 16
KOUT = 64
TOK = 128
GROUP = 128
DC = 512
NC = WIDTH // DC
GPC = DC // GROUP
PR = DC // 4
HROWS = 96
NORM = 32768.0**-0.5


def mm(a, b, ca, cb):
    return lax.dot_general(a, b, (((ca,), (cb,)), ((), ())), preferred_element_type=F32)


def iota(shape, dim):
    return lax.broadcasted_iota(jnp.int32, shape, dim)


def eye(n):
    return (iota((n, n), 0) == iota((n, n), 1)).astype(BF16)


def unshuffle():
    q, d = iota((GROUP, GROUP), 0), iota((GROUP, GROUP), 1)
    return (d == 4 * (q & 31) + (q >> 5)).astype(BF16)


def kernel(
    act_h, g_h, pk_h, scale, idx, dfw, a_h, up,
    out_h, out_d, out_u, out_o,
    act, g, pk, a_v, at, w, rank, rank_in, r_v, hid, dsum, dbuf, dall, usum, ubuf, uall,
    s1, r1, s2, r2, sz, rz, own, outv,
    l_sem, pk_sem, o_sem, s1s, s1r, s2s, s2r, zs, zr, rks, rkr, hs, hr, ds, dr, us, ur,
):
    dp = lax.axis_index("dp")
    t = lax.axis_index("tensor")
    core = lax.rem(dp, 2)
    y = dp // 8
    zl = lax.rem(dp // 2, 4)
    x = t // 2
    zh = lax.rem(t, 2)
    z = zh * 4 + zl

    def at_t(d):
        return (dp, lax.rem(t + d, 8))

    def at_x(d):
        return (dp, lax.rem(x + d + 4, 4) * 2 + zh)

    def at_y(d):
        return ((lax.rem(y + d, 4) * 4 + zl) * 2 + core, t)

    def at_z(d):
        zz = lax.rem(z + d, 8)
        return ((y * 4 + lax.rem(zz, 4)) * 2 + core, x * 2 + zz // 4)

    def at_zl(d):
        return ((y * 4 + lax.rem(zl + d, 4)) * 2 + core, t)

    sibling = (dp + 1 - 2 * core, t)

    def rc(src, dst, ssem, rsem, dev):
        return pltpu.make_async_remote_copy(
            src_ref=src, dst_ref=dst, send_sem=ssem, recv_sem=rsem,
            device_id=dev, device_id_type=MESH,
        )

    bar = pltpu.get_barrier_semaphore()
    peers = [at_t(d) for d in range(1, 8)]
    peers += [at_y(d) for d in range(1, 4)]
    peers += [at_z(d) for d in (1, 2, 3, 5, 6, 7)]
    peers += [sibling]
    for dev in peers:
        pl.semaphore_signal(bar, inc=1, device_id=dev, device_id_type=MESH)

    cp_g = pltpu.make_async_copy(g_h, g, l_sem.at[0])
    cp_act = pltpu.make_async_copy(act_h, act, l_sem.at[1])
    cp_a = pltpu.make_async_copy(a_h, a_v, l_sem.at[2])

    def cp_pk(j):
        return pltpu.make_async_copy(
            pk_h.at[pl.ds(j * PR, PR)], pk.at[j], pk_sem.at[j]
        )

    cp_g.start()
    for j in range(2):
        cp_pk(j).start()
    cp_act.start()
    cp_a.start()
    for j in range(2, NC):
        cp_pk(j).start()
    cp_g.wait()

    def unpack(j):
        cp_pk(j).wait()
        slot = lax.rem(j, 3)
        for q in range(GPC):
            k = j * GPC + q
            words = pk[j, pl.ds(q * 32, 32), :]
            srow = scale[pl.ds(k, 1), :]
            drow = dfw[pl.ds(k, 1), :]
            place = idx[pl.ds(k, 1), :] - k * GROUP
            place = (place & 3) * 32 + (place >> 2)
            for n in range(4):
                code = lax.shift_right_logical(words, 4 * n) & 15
                val = (code.astype(F32) - 8.0) * srow
                hit = iota((32, FEATS), 0) + n * 32 == place
                val = val + jnp.where(hit, drow, 0.0)
                w[slot, pl.ds(q * GROUP + n * 32, 32), :] = val.astype(BF16)

    def part(j, xx):
        rows = g[pl.ds(pl.multiple_of(xx * 256, 256), 256), :]
        return mm(rows, w[lax.rem(j, 3)], 1, 1)

    def c1(j, i):
        return rc(s1.at[j, i], r1.at[j, i], s1s.at[j, i], s1r.at[j, i], at_x(1 - 2 * i))

    def c2(j, i):
        return rc(s2.at[j, i], r2.at[j, i], s2s.at[j, i], s2r.at[j, i], at_x(1 - 2 * i))

    def cz(j):
        return rc(sz.at[j], rz.at[j], zs.at[j], zr.at[j], at_z(4))

    def stage1(j):
        p = part(j, lax.rem(x + 2, 4)).astype(BF16)
        s1[j, 0] = p[:TOK]
        s1[j, 1] = p[TOK:]

    def stage2(j):
        for i in range(2):
            p = part(j, lax.rem(x + 5 - 2 * i, 4))
            c1(j, i).wait_recv()
            got = r1[j, i].astype(F32)
            lo, hi = p[:TOK], p[TOK:]
            if i == 0:
                lo = lo + got
            else:
                hi = hi + got
            s2[j, i, pl.ds(0, TOK), :] = lo.astype(BF16)
            s2[j, i, pl.ds(TOK, TOK), :] = hi.astype(BF16)
            c2(j, i).start()

    def stage3(j):
        p = part(j, x)
        c2(j, 0).wait_recv()
        c2(j, 1).wait_recv()
        p = p + r2[j, 0].astype(F32) + r2[j, 1].astype(F32)
        first = zh == 0
        own[j] = jnp.where(first, p[:TOK], p[TOK:])
        sz[j] = jnp.where(first, p[TOK:], p[:TOK]).astype(BF16)
        cz(j).start()

    def out_copy(j):
        cols = pl.ds(pl.multiple_of(j * DC, DC), DC)
        return pltpu.make_async_copy(outv.at[j], out_h.at[:, cols], o_sem.at[j])

    def stage4(j):
        shuf = unshuffle()
        cols = at[:, pl.ds(pl.multiple_of(j * DC, DC), DC)]
        cz(j).wait_recv()
        for q in range(GPC):
            lanes = slice(q * GROUP, (q + 1) * GROUP)
            a_q = mm(cols[:, lanes], shuf, 1, 1).astype(BF16)
            total = own[j, :, lanes] + rz[j, :, lanes].astype(F32)
            total = total + mm(r_v[...], a_q, 1, 0)
            outv[j, :, lanes] = mm(total.astype(BF16), shuf, 1, 0).astype(BF16)
        out_copy(j).start()

    def c_rank(d):
        return rc(rank.at[lax.rem(t + d, 8)], rank_in.at[t], rks.at[d], rkr.at[d], at_t(d))

    def c_hid(d):
        return rc(hid.at[t], hid.at[t], hs.at[d], hr.at[d], at_t(d))

    def cd_core():
        return rc(dsum.at[1 - core], dbuf.at[pl.ds(0, 16)], ds.at[0], dr.at[0], sibling)

    def cu_core():
        return rc(usum.at[1 - core], ubuf.at[pl.ds(0, 4)], us.at[0], ur.at[0], sibling)

    def cd_x(d):
        to = lax.rem(x + d, 4)
        src = dsum.at[core, pl.ds(to * 4, 4)]
        return rc(src, dbuf.at[pl.ds(16 + 4 * (d - 1), 4)], ds.at[d], dr.at[d], at_x(d))

    def cd_y(d):
        src = dsum.at[core, x * 4 + lax.rem(y + d, 4)]
        return rc(src, dbuf.at[28 + d - 1], ds.at[3 + d], dr.at[3 + d], at_y(d))

    def cd_z(d):
        return rc(dbuf.at[31 + z], dbuf.at[31 + z], ds.at[6 + d], dr.at[6 + d], at_z(d))

    def cu_y(d):
        src = usum.at[core, lax.rem(y + d, 4)]
        return rc(src, ubuf.at[4 + d - 1], us.at[d], ur.at[d], at_y(d))

    def cu_z(d):
        return rc(ubuf.at[7 + zl], ubuf.at[7 + zl], us.at[3 + d], ur.at[3 + d], at_zl(d))

    def cd_gy(d):
        ref = dall.at[core, x * 4 + y]
        return rc(ref, ref, ds.at[13 + d], dr.at[13 + d], at_y(d))

    def cd_gx(d):
        ref = dall.at[core, pl.ds(x * 4, 4)]
        return rc(ref, ref, ds.at[16 + d], dr.at[16 + d], at_x(d))

    def cd_gc():
        ref = dall.at[core]
        return rc(ref, ref, ds.at[20], dr.at[20], sibling)

    def cu_gy(d):
        ref = uall.at[core, y]
        return rc(ref, ref, us.at[6 + d], ur.at[6 + d], at_y(d))

    def cu_gc():
        ref = uall.at[core]
        return rc(ref, ref, us.at[10], ur.at[10], sibling)

    r13, r17 = range(1, 4), range(1, 8)

    def small0():
        part_r = mm(up[...], g[...], 1, 1)
        for k in range(8):
            rank[k] = part_r[:, k * TOK:(k + 1) * TOK]
        rank_in[t] = rank[t]
        for d in r17:
            c_rank(d).start()
        cp_act.wait()
        cp_a.wait()
        e16 = eye(RANK)
        total = jnp.zeros((HROWS, TOK), F32)
        step = 1024
        for c in range(WIDTH // step):
            cols = slice(c * step, (c + 1) * step)
            a_c = mm(e16, a_v[cols, :], 1, 1).astype(BF16)
            at[:, cols] = a_c
            hot = (iota((KOUT, step), 1) + c * step == idx[...]).astype(F32).astype(BF16)
            zero = jnp.zeros((HROWS - RANK - KOUT, step), BF16)
            basis = jnp.concatenate([a_c, hot, zero], axis=0)
            total = total + mm(basis, act[:, cols], 1, 1)
        hid[t] = total.astype(BF16)
        for d in r17:
            c_hid(d).start()

    def small1():
        for d in r17:
            c_rank(d).wait_recv()
        total = rank_in[0]
        for k in range(1, 8):
            total = total + rank_in[k]
        r_t = (2.0 * total).astype(BF16)
        r_v[...] = mm(eye(TOK), r_t, 1, 1).astype(BF16)
        for k in range(32):
            cols = slice(k * 256, (k + 1) * 256)
            dsum[k // 16, k % 16] = mm(r_t, act[:, cols], 1, 0)
        cd_core().start()

    def small2():
        for d in r17:
            c_hid(d).wait_recv()
        total = jnp.zeros((HROWS, FEATS), F32)
        for k in range(8):
            total = total + mm(hid[k], g[k * TOK:(k + 1) * TOK, :], 1, 0)
        for c in range(2):
            for k in range(4):
                usum[c, k] = total[k * 24:(k + 1) * 24, c * 384:(c + 1) * 384]
        cu_core().start()

    def small3():
        cd_core().wait_recv()
        for k in range(16):
            dsum[core, k] = dsum[core, k] + dbuf[k]
        for d in r13:
            cd_x(d).start()
        cu_core().wait_recv()
        for k in range(4):
            usum[core, k] = usum[core, k] + ubuf[k]
        for d in r13:
            cu_y(d).start()

    def small4():
        for d in r13:
            cd_x(d).wait_recv()
        for k in range(4):
            mine = dsum[core, x * 4 + k]
            for d in r13:
                mine = mine + dbuf[16 + 4 * (d - 1) + k]
            dsum[core, x * 4 + k] = mine
        for d in r13:
            cd_y(d).start()
        for d in r13:
            cu_y(d).wait_recv()
        mine = usum[core, y]
        for d in r13:
            mine = mine + ubuf[4 + d - 1]
        ubuf[7 + zl] = mine
        for d in r13:
            cu_z(d).start()

    def small5():
        for d in r13:
            cd_y(d).wait_recv()
        mine = dsum[core, x * 4 + y]
        for d in r13:
            mine = mine + dbuf[28 + d - 1]
        dbuf[31 + z] = mine
        for d in r17:
            cd_z(d).start()
        for d in r13:
            cu_z(d).wait_recv()
        total = ubuf[7]
        for k in r13:
            total = total + ubuf[7 + k]
        uall[core, y] = total
        for d in r13:
            cu_gy(d).start()

    def small6():
        for d in r17:
            cd_z(d).wait_recv()
        total = dbuf[31]
        for k in range(1, 8):
            total = total + dbuf[31 + k]
        dall[core, x * 4 + y] = total * NORM
        for d in r13:
            cd_gy(d).start()
        for d in r13:
            cu_gy(d).wait_recv()
        cu_gc().start()

    def small7():
        for d in r13:
            cd_gy(d).wait_recv()
        for d in r13:
            cd_gx(d).start()
        cu_gc().wait_recv()
        for c in range(2):
            lanes = slice(c * 384, (c + 1) * 384)
            u0 = uall[c, 0]
            out_u[:, lanes] = u0[:16] * (2.0 * NORM)
            out_o[0:8, lanes] = u0[16:] * NORM
            out_o[8:32, lanes] = uall[c, 1] * NORM
            out_o[32:56, lanes] = uall[c, 2] * NORM
            out_o[56:64, lanes] = uall[c, 3, :8] * NORM

    def small8():
        for d in r13:
            cd_gx(d).wait_recv()
        cd_gc().start()

    def small9():
        cd_gc().wait_recv()
        for c in range(2):
            for k in range(16):
                out_d[c * 16 + k] = dall[c, k]

    unpack(0)
    stage1(0)
    pl.semaphore_wait(bar, len(peers))
    for i in range(2):
        c1(0, i).start()
    small0()

    small = {2: small1, 3: small2, 4: small3, 5: small4, 6: small5, 7: small6,
             8: small7, 9: small8, 10: small9}

    def step(j, carry):
        @pl.when(j < NC)
        def _():
            unpack(j)
            stage1(j)
            for i in range(2):
                c1(j, i).start()

        @pl.when(j <= NC)
        def _():
            stage2(j - 1)

        @pl.when((j >= 2) & (j <= NC + 1))
        def _():
            stage3(j - 2)

        @pl.when(j >= 4)
        def _():
            stage4(j - 4)

        for at_step, piece in small.items():
            pl.when(j == at_step)(piece)
        return carry

    lax.fori_loop(1, NC + 4, step, 0)

    def drain(j, carry):
        for i in range(2):
            c1(j, i).wait_send()
            c2(j, i).wait_send()
        cz(j).wait_send()
        out_copy(j).wait()
        return carry

    lax.fori_loop(0, NC, drain, 0)
    for d in r17:
        c_rank(d).wait_send()
        c_hid(d).wait_send()
        cd_z(d).wait_send()
    for d in r13:
        cd_x(d).wait_send()
        cd_y(d).wait_send()
        cu_y(d).wait_send()
        cu_z(d).wait_send()
        cd_gy(d).wait_send()
        cd_gx(d).wait_send()
        cu_gy(d).wait_send()
    cd_core().wait_send()
    cu_core().wait_send()
    cd_gc().wait_send()
    cu_gc().wait_send()


def body(act, g, pk, scale, idx, dfw, a, up):
    hbm = pl.BlockSpec(memory_space=pl.ANY)
    vmem = pl.BlockSpec(memory_space=pltpu.VMEM)
    dma = pltpu.SemaphoreType.DMA
    out, d, u, o = pl.pallas_call(
        kernel,
        out_shape=(
            jax.ShapeDtypeStruct((TOK, WIDTH), BF16),
            jax.ShapeDtypeStruct((32, RANK, 256), F32),
            jax.ShapeDtypeStruct((RANK, FEATS), F32),
            jax.ShapeDtypeStruct((KOUT, FEATS), F32),
        ),
        in_specs=[hbm, hbm, hbm, vmem, vmem, vmem, hbm, vmem],
        out_specs=(hbm, vmem, vmem, vmem),
        scratch_shapes=[
            pltpu.VMEM((TOK, WIDTH), BF16),
            pltpu.VMEM((8 * TOK, FEATS), BF16),
            pltpu.VMEM((NC, PR, FEATS), jnp.int32),
            pltpu.VMEM((WIDTH, RANK), BF16),
            pltpu.VMEM((RANK, WIDTH), BF16),
            pltpu.VMEM((3, DC, FEATS), BF16),
            pltpu.VMEM((8, RANK, TOK), F32),
            pltpu.VMEM((8, RANK, TOK), F32),
            pltpu.VMEM((TOK, RANK), BF16),
            pltpu.VMEM((8, HROWS, TOK), BF16),
            pltpu.VMEM((2, 16, RANK, 256), F32),
            pltpu.VMEM((39, RANK, 256), F32),
            pltpu.VMEM((2, 16, RANK, 256), F32),
            pltpu.VMEM((2, 4, 24, 384), F32),
            pltpu.VMEM((11, 24, 384), F32),
            pltpu.VMEM((2, 4, 24, 384), F32),
            pltpu.VMEM((NC, 2, TOK, DC), BF16),
            pltpu.VMEM((NC, 2, TOK, DC), BF16),
            pltpu.VMEM((NC, 2, 2 * TOK, DC), BF16),
            pltpu.VMEM((NC, 2, 2 * TOK, DC), BF16),
            pltpu.VMEM((NC, TOK, DC), BF16),
            pltpu.VMEM((NC, TOK, DC), BF16),
            pltpu.VMEM((NC, TOK, DC), F32),
            pltpu.VMEM((NC, TOK, DC), BF16),
            dma((3,)), dma((NC,)), dma((NC,)),
            dma((NC, 2)), dma((NC, 2)), dma((NC, 2)), dma((NC, 2)),
            dma((NC,)), dma((NC,)),
            dma((8,)), dma((8,)), dma((8,)), dma((8,)),
            dma((21,)), dma((21,)), dma((11,)), dma((11,)),
        ],
        compiler_params=pltpu.CompilerParams(
            collective_id=0, has_side_effects=True, vmem_limit_bytes=60 << 20
        ),
        name="projection_backward",
    )(act, g, pk, scale, idx.reshape(KOUT, 1), dfw, a, up)
    return out, d.transpose(0, 2, 1).reshape(WIDTH, RANK), u, o


def solution(mesh):
    tensor = P(None, "tensor")
    tokens = P(("dp", "tensor"), None)
    return jax.shard_map(
        body,
        mesh=mesh,
        in_specs=(tokens, P("dp", "tensor"), tensor, tensor, P(), tensor, P(), tensor),
        out_specs=(tokens, P(), tensor, tensor),
        check_vma=False,
    )
```

time: 1340 us -> 181 us (0.14); the launches traced: 1320 us -> 181 us
  waiting for transfers between devices: 848 us -> 0 us
  Pallas kernels: 0 us -> 170 us
  local copies, waits for them, and re-layouts: 165 us -> 10.2 us
  blocking collectives: 153 us -> 0 us
  other arithmetic: 93.5 us -> 0 us
  matrix products: 41.2 us -> 0 us
    psum x3 -> x0, waiting for transfers between devices: 516 us -> none  [the longest x1 266 us: body(): lax.psum(grad_norm * contract_leading(activations, local_rank_slice), ('d...]
    reduce_scatter x1 -> x0, waiting for transfers between devices: 174 us -> none  [body(): lax.psum_scatter(partial_value.at[:, dense_feature_index].add(outlier_ter...]
    pallas_call x0 -> x1, Pallas kernels: none -> 170 us  [body(): pl.pallas_call(kernel, out_shape=(jax.ShapeDtypeStruct((TOK, WIDTH), BF16...]
    all_gather x1 -> x0, waiting for transfers between devices: 159 us -> none  [body(): block_row_span = lax.all_gather(activations, 'tensor', axis=0, tiled=True)]
    psum x1 -> x0, blocking collectives: 153 us -> none  [body(): lax.psum((grad_norm * up_gradient_total, grad_norm * outlier_total), 'dp')]
    shift_right_arithmetic x320 -> x0, local copies, waits for them, and re-layouts: 77.4 us -> none  [one_group(): jnp.right_shift(packed[:, None, :], shifts[None, :, None])]
    dynamic_update_slice x64 -> x0, other arithmetic: 52.7 us -> none  [unpack(): lax.map(one_group, (blocks, group_scale_table)).reshape(total_rows, columns)]
    dynamic_slice x64 -> x0, local copies, waits for them, and re-layouts: 48.6 us -> none  [unpack(): lax.map(one_group, (blocks, group_scale_table)).reshape(total_rows, columns)]
  transfers between devices with their start and end apart: 5 -> 0, of which waited for: 4 -> 0; matrix products, arithmetic and copies ran while one was open for 22% -> 0% of each run, Pallas kernels for 0% -> 0%
where the time goes in v1:
time: 181 us
  Pallas kernels  170 us (94%)
  local copies, waits for them, and re-layouts  10.2 us (6%)
    pallas_call x1, Pallas kernels, body(): pl.pallas_call(kernel, out_shape=(jax.ShapeDtypeStruct((TOK, WIDTH), BF16...  170 us
    unnamed x8, local copies, waits for them, and re-layouts  7.01 us

profile of v1, /device:TPU:16, one launch (start us, length us, event | category | flops | bytes accessed | tf_op | source)
XLA Modules:
  0.0 180.7 jit_solution(2765691787016138227)
XLA Ops:
  0.6 1.4 copy.14.idx
  2.0 2.6 %copy.15.a_h = bf16[8192,16]{1,0:T(8,128)(2,1)} copy(bf16[8192,16]{0,1:T(8,128)(2,1)} %param.14) | data formatting | bytes 524288 | tf_op args[6]
  4.6 169.9 %projection_backward.1 = (bf16[128,8192]{1,0:T(8,128)(2,1)}, f32[32,16,256]{2,1,0:T(8,128)}, f32[16,768]{1,0:T(8,128)}, f32[64,768]{1,0:T(8,128)}) custom-call(bf16[128,8192]{1,0:T(8,128)(2,1)} %act_h.1, bf16[1024,768]{1,0:T(8,128)(2,1)} %g_h.1, s32[2048,768]{1,0:T(8,128)} %pk_h.1, f32[64,768]{1,0:T(8,128)} %scale.1, s32[64,1]{1,0:T(8,128)} %copy.14.idx, ...), custom_call_target="tpu_custom_call" | custom-call | tf_op jit(solution)/shard_map/projection_backward/pallas_call | solution.py:442
  174.4 1.9 %copy.17 = f32[32,2,8,256]{3,2,0,1:T(8,128)} copy(f32[32,2,8,256]{3,2,1,0:T(8,128)} %bitcast.5) | data formatting | bytes 1048576 | tf_op jit(solution)/shard_map/reshape | solution.py:488
  176.3 0.0 copy-start.1
  176.3 0.0 copy-start
  176.3 3.1 %copy.21 = bf16[128,8192]{1,0:T(8,128)(2,1)} copy(bf16[128,8192]{1,0:T(8,128)(2,1)} %get-tuple-element.16) | data formatting | bytes 4194304
  179.4 0.0 copy-done.1
  179.4 0.6 copy.22
  180.1 0.0 copy-done
  180.1 0.7 copy.23
Async XLA Ops:
  176.3 3.1 %copy-start.1 = (f32[16,768]{1,0:T(8,128)S(1)}, f32[16,768]{1,0:T(8,128)}, u32[]{:S(2)}) copy-start(f32[16,768]{1,0:T(8,128)} %get-tuple-element.18) | copy-start | bytes 147460
  176.3 3.8 %copy-start = (f32[64,768]{1,0:T(8,128)S(1)}, f32[64,768]{1,0:T(8,128)}, u32[]{:S(2)}) copy-start(f32[64,768]{1,0:T(8,128)} %get-tuple-element.19) | copy-start | bytes 589828

commit v2 on v1

--- a/solution.py
+++ b/solution.py
@@ -21,6 +21,12 @@
 NC = WIDTH // DC
 GPC = DC // GROUP
 PR = DC // 4
+NA = 7
+NB = NC - NA
+S2 = 2
+S3 = 4
+CUTS = (0, 2, 5, 9)
+PK = 6
 HROWS = 96
 NORM = 32768.0**-0.5
 
@@ -43,11 +49,12 @@
 
 
 def kernel(
-    act_h, g_h, pk_h, scale, idx, dfw, a_h, up,
+    act_h, g_h, pk_h, scale, idx_row, dfw, at, up,
     out_h, out_d, out_u, out_o,
-    act, g, pk, a_v, at, w, rank, rank_in, r_v, hid, dsum, dbuf, dall, usum, ubuf, uall,
-    s1, r1, s2, r2, sz, rz, own, outv,
-    l_sem, pk_sem, o_sem, s1s, s1r, s2s, s2r, zs, zr, rks, rkr, hs, hr, ds, dr, us, ur,
+    act, g, gb, gp, pka, pkb, idx, atp, w, wp, rank, rank_in, r_v, hid, dsum, dbuf, dall, usum, ubuf, uall,
+    s1, r1, s2, r2, sz, rz, own, t1, q1, t2, q2, near, home, outv,
+    l_sem, pka_sem, pkb_sem, o_sem, s1s, s1r, s2s, s2r, zs, zr, t1s, t1r, t2s, t2r, gs, gr,
+    wzs, wzr, wfs, wys, wyr, wcs, wcr, rks, rkr, hs, hr, ds, dr, us, ur,
 ):
     dp = lax.axis_index("dp")
     t = lax.axis_index("tensor")
@@ -92,28 +99,33 @@
 
     cp_g = pltpu.make_async_copy(g_h, g, l_sem.at[0])
     cp_act = pltpu.make_async_copy(act_h, act, l_sem.at[1])
-    cp_a = pltpu.make_async_copy(a_h, a_v, l_sem.at[2])
-
-    def cp_pk(j):
-        return pltpu.make_async_copy(
-            pk_h.at[pl.ds(j * PR, PR)], pk.at[j], pk_sem.at[j]
-        )
+
+    def cp_a(j):
+        return pltpu.make_async_copy(pk_h.at[pl.ds(j * PR, PR)], pka.at[j], pka_sem.at[j])
+
+    def cp_b(b):
+        slot = lax.rem(b, PK)
+        src = pk_h.at[pl.ds((NA + b) * PR, PR)]
+        return pltpu.make_async_copy(src, pkb.at[slot], pkb_sem.at[slot])
 
     cp_g.start()
-    for j in range(2):
-        cp_pk(j).start()
+    cp_a(0).start()
+    cp_b(0).start()
+    for j in range(1, NA):
+        cp_a(j).start()
     cp_act.start()
-    cp_a.start()
-    for j in range(2, NC):
-        cp_pk(j).start()
-    cp_g.wait()
-
-    def unpack(j):
-        cp_pk(j).wait()
-        slot = lax.rem(j, 3)
+    for b in range(1, PK):
+        cp_b(b).start()
+    row = idx_row[...].astype(F32)
+    idx[...] = jnp.sum(
+        jnp.where(iota((KOUT, KOUT), 0) == iota((KOUT, KOUT), 1), row, 0.0),
+        axis=1, keepdims=True,
+    ).astype(jnp.int32)
+
+    def unpack(j, packed):
         for q in range(GPC):
             k = j * GPC + q
-            words = pk[j, pl.ds(q * 32, 32), :]
+            words = packed[pl.ds(q * 32, 32), :]
             srow = scale[pl.ds(k, 1), :]
             drow = dfw[pl.ds(k, 1), :]
             place = idx[pl.ds(k, 1), :] - k * GROUP
@@ -123,11 +135,23 @@
                 val = (code.astype(F32) - 8.0) * srow
                 hit = iota((32, FEATS), 0) + n * 32 == place
                 val = val + jnp.where(hit, drow, 0.0)
-                w[slot, pl.ds(q * GROUP + n * 32, 32), :] = val.astype(BF16)
+                w[j, pl.ds(q * GROUP + n * 32, 32), :] = val.astype(BF16)
+
+    def unpack_a(j):
+        cp_a(j).wait()
+        unpack(j, pka.at[j])
+
+    def unpack_b(b):
+        cp_b(b).wait()
+        unpack(NA + b, pkb.at[lax.rem(b, PK)])
+
+        @pl.when(b + PK < NB)
+        def _():
+            cp_b(b + PK).start()
 
     def part(j, xx):
         rows = g[pl.ds(pl.multiple_of(xx * 256, 256), 256), :]
-        return mm(rows, w[lax.rem(j, 3)], 1, 1)
+        return mm(rows, w[j], 1, 1)
 
     def c1(j, i):
         return rc(s1.at[j, i], r1.at[j, i], s1s.at[j, i], s1r.at[j, i], at_x(1 - 2 * i))
@@ -165,23 +189,109 @@
         first = zh == 0
         own[j] = jnp.where(first, p[:TOK], p[TOK:])
         sz[j] = jnp.where(first, p[TOK:], p[:TOK]).astype(BF16)
-        cz(j).start()
 
     def out_copy(j):
         cols = pl.ds(pl.multiple_of(j * DC, DC), DC)
         return pltpu.make_async_copy(outv.at[j], out_h.at[:, cols], o_sem.at[j])
 
-    def stage4(j):
+    def finish(j, total):
         shuf = unshuffle()
-        cols = at[:, pl.ds(pl.multiple_of(j * DC, DC), DC)]
-        cz(j).wait_recv()
+        cols = atp[:, pl.ds(pl.multiple_of(j * DC, DC), DC)]
+        full = (total + mm(r_v[...], cols, 1, 0)).astype(BF16)
         for q in range(GPC):
             lanes = slice(q * GROUP, (q + 1) * GROUP)
-            a_q = mm(cols[:, lanes], shuf, 1, 1).astype(BF16)
-            total = own[j, :, lanes] + rz[j, :, lanes].astype(F32)
-            total = total + mm(r_v[...], a_q, 1, 0)
-            outv[j, :, lanes] = mm(total.astype(BF16), shuf, 1, 0).astype(BF16)
+            outv[j, :, lanes] = mm(full[:, lanes], shuf, 1, 0).astype(BF16)
         out_copy(j).start()
+
+    def stage4(j):
+        cz(j).wait_recv()
+        finish(j, own[j] + rz[j].astype(F32))
+
+    order = (2, 1, 3, 0)
+
+    def block(d, half):
+        return pl.ds(pl.multiple_of((lax.rem(x + d, 4) * 2 + half) * TOK, TOK), TOK)
+
+    def c_g(k):
+        dst = gp.at[pl.ds(k * TOK, TOK)]
+        return rc(g.at[block(order[k], 1 - zh)], dst, gs.at[k], gr.at[k], at_z(4))
+
+    def piece(b, k):
+        return wp.at[b, pl.ds(pl.multiple_of(core * 256 + k * 64, 64), 64)]
+
+    outer = (zl == 0) | (zl == 3)
+
+    def c_wz(b):
+        src = w.at[NA + b, pl.ds(pl.multiple_of(core * 256 + y * 64, 64), 64)]
+        return rc(src, piece(b, y), wzs.at[b], wzr.at[b], at_z(7 - 2 * zl))
+
+    def c_wf(b):
+        return rc(piece(b, y), piece(b, y), wfs.at[b], wzr.at[b], at_z(1 + 2 * zl))
+
+    def c_wy(b, d):
+        return rc(piece(b, y), piece(b, y), wys.at[b, d - 1], wyr.at[b, d - 1], at_y(d))
+
+    def c_wc(b):
+        ref = wp.at[b, pl.ds(pl.multiple_of(core * 256, 256), 256)]
+        return rc(ref, ref, wcs.at[b], wcr.at[b], sibling)
+
+    def spread(b):
+        c_wz(b).wait_recv()
+        for d in (1, 3, 2):
+            c_wy(b, d).start()
+
+    def weight_send(b):
+        pl.when(outer)(lambda: c_wz(b).start())
+
+    def weight_on(b):
+        @pl.when(outer)
+        def _():
+            c_wz(b).wait_recv()
+            c_wf(b).start()
+            for d in (1, 3, 2):
+                c_wy(b, d).start()
+
+    def weight_in(b):
+        pl.when(jnp.logical_not(outer))(lambda: spread(b))
+
+    def weight_pair(b):
+        for d in (1, 3, 2):
+            c_wy(b, d).wait_recv()
+        c_wc(b).start()
+
+    def d1(b, i):
+        return rc(t1.at[b, i], q1.at[b, i], t1s.at[b, i], t1r.at[b, i], at_x(1 - 2 * i))
+
+    def d2(b, i):
+        return rc(t2.at[b, i], q2.at[b, i], t2s.at[b, i], t2r.at[b, i], at_x(1 - 2 * i))
+
+    def both1(b):
+        c_wc(b).wait_recv()
+        p = mm(gb[...], w[NA + b], 1, 1) + mm(gp[...], wp[b], 1, 1)
+        far = p[:TOK].astype(BF16)
+        t1[b, 0] = far[:64]
+        t1[b, 1] = far[64:]
+        near[lax.rem(b, S2 + 1)] = p[TOK:3 * TOK]
+        home[lax.rem(b, S3 + 1)] = p[3 * TOK:]
+        for i in range(2):
+            d1(b, i).start()
+
+    def both2(b):
+        p = near[lax.rem(b, S2 + 1)]
+        d1(b, 0).wait_recv()
+        t2[b, 0, pl.ds(0, 64), :] = (p[:64] + q1[b, 0].astype(F32)).astype(BF16)
+        t2[b, 0, pl.ds(64, 64), :] = p[64:128].astype(BF16)
+        d2(b, 0).start()
+        d1(b, 1).wait_recv()
+        t2[b, 1, pl.ds(0, 64), :] = p[128:192].astype(BF16)
+        t2[b, 1, pl.ds(64, 64), :] = (p[192:] + q1[b, 1].astype(F32)).astype(BF16)
+        d2(b, 1).start()
+
+    def both3(b):
+        p = home[lax.rem(b, S3 + 1)]
+        d2(b, 0).wait_recv()
+        d2(b, 1).wait_recv()
+        finish(NA + b, p + q2[b, 0].astype(F32) + q2[b, 1].astype(F32))
 
     def c_rank(d):
         return rc(rank.at[lax.rem(t + d, 8)], rank_in.at[t], rks.at[d], rkr.at[d], at_t(d))
@@ -244,14 +354,11 @@
         for d in r17:
             c_rank(d).start()
         cp_act.wait()
-        cp_a.wait()
-        e16 = eye(RANK)
         total = jnp.zeros((HROWS, TOK), F32)
         step = 1024
         for c in range(WIDTH // step):
             cols = slice(c * step, (c + 1) * step)
-            a_c = mm(e16, a_v[cols, :], 1, 1).astype(BF16)
-            at[:, cols] = a_c
+            a_c = at[:, cols]
             hot = (iota((KOUT, step), 1) + c * step == idx[...]).astype(F32).astype(BF16)
             zero = jnp.zeros((HROWS - RANK - KOUT, step), BF16)
             basis = jnp.concatenate([a_c, hot, zero], axis=0)
@@ -259,6 +366,17 @@
         hid[t] = total.astype(BF16)
         for d in r17:
             c_hid(d).start()
+
+    def arrange():
+        shuf = unshuffle()
+        for c in range(8):
+            groups = [at[:, (c * 8 + k) * GROUP:(c * 8 + k + 1) * GROUP] for k in range(8)]
+            moved = mm(jnp.concatenate(groups, axis=0), shuf, 1, 1).astype(BF16)
+            for k in range(8):
+                lanes = slice((c * 8 + k) * GROUP, (c * 8 + k + 1) * GROUP)
+                atp[:, lanes] = moved[k * RANK:(k + 1) * RANK]
+        for k in range(4):
+            gb[k * TOK:(k + 1) * TOK, :] = g[block(order[k], zh), :]
 
     def small1():
         for d in r17:
@@ -370,53 +488,97 @@
         cd_gc().wait_recv()
         for c in range(2):
             for k in range(16):
-                out_d[c * 16 + k] = dall[c, k]
-
-    unpack(0)
+                out_d[:, (c * 16 + k) * 256:(c * 16 + k + 1) * 256] = dall[c, k]
+
+    unpack_a(0)
+    cp_g.wait()
     stage1(0)
     pl.semaphore_wait(bar, len(peers))
     for i in range(2):
         c1(0, i).start()
     small0()
-
-    small = {2: small1, 3: small2, 4: small3, 5: small4, 6: small5, 7: small6,
-             8: small7, 9: small8, 10: small9}
+    for k in range(4):
+        c_g(k).start()
+
+    small = {0: arrange, 2: small1, 3: small2, 4: small3, 6: small4, 8: small5, 12: small6,
+             14: small7, 15: small8, 16: small9}
+
+    def batch(k, todo):
+        hi = NB if k == len(CUTS) - 2 else CUTS[k + 1]
+        lax.fori_loop(CUTS[k], hi, lambda b, c: (todo(b), c)[1], 0)
+
+    def serve(n):
+        for k in range(len(CUTS) - 1):
+            for after, todo in ((2, weight_in), (1, weight_on), (0, weight_send)):
+                pl.when(n == k + after)(functools.partial(batch, k, todo))
 
     def step(j, carry):
-        @pl.when(j < NC)
+        j2, j3 = j - S2, j - S3
+        pl.when((j2 >= 0) & (j2 < NA))(lambda: stage2(j2))
+        pl.when((j2 >= NA) & (j2 < NC))(lambda: both2(j2 - NA))
+        b = j - NA
+        pl.when((b >= 0) & (b < NB))(lambda: weight_pair(b))
+        serve(2 * (j - NA) + 3)
+        pl.when((j3 >= 0) & (j3 < NA))(lambda: stage3(j3))
+        pl.when(j3 >= NA)(lambda: both3(j3 - NA))
+
+        @pl.when(j == NA - 2)
         def _():
-            unpack(j)
+            for k in range(4):
+                c_g(k).wait_recv()
+
+        serve(2 * (j - NA) + 4)
+
+        @pl.when((j >= 1) & (j < NA))
+        def _():
+            unpack_a(j)
             stage1(j)
             for i in range(2):
                 c1(j, i).start()
 
-        @pl.when(j <= NC)
-        def _():
-            stage2(j - 1)
-
-        @pl.when((j >= 2) & (j <= NC + 1))
-        def _():
-            stage3(j - 2)
-
-        @pl.when(j >= 4)
-        def _():
-            stage4(j - 4)
-
-        for at_step, piece in small.items():
-            pl.when(j == at_step)(piece)
+        ahead = 2 * j
+        for k in range(2):
+            pl.when((ahead >= 0) & (ahead + k < NB))(lambda: unpack_b(ahead + k))
+        pl.when((j >= NA) & (j < NC))(lambda: both1(j - NA))
+
+        late = j - NA - 1
+        pl.when((late >= 0) & (late < NA))(lambda: cz(late).start())
+
+        for at_step, todo in small.items():
+            pl.when(j == at_step)(todo)
         return carry
 
-    lax.fori_loop(1, NC + 4, step, 0)
-
-    def drain(j, carry):
+    lax.fori_loop(0, NC + S3, step, 0)
+    lax.fori_loop(0, NA, lambda a, c: (stage4(a), c)[1], 0)
+
+    def drain_a(j, carry):
         for i in range(2):
             c1(j, i).wait_send()
             c2(j, i).wait_send()
         cz(j).wait_send()
-        out_copy(j).wait()
         return carry
 
-    lax.fori_loop(0, NC, drain, 0)
+    def drain_b(b, carry):
+        for i in range(2):
+            d1(b, i).wait_send()
+            d2(b, i).wait_send()
+        for d in r13:
+            c_wy(b, d).wait_send()
+        c_wc(b).wait_send()
+
+
+        @pl.when(outer)
+        def _():
+            c_wz(b).wait_send()
+            c_wf(b).wait_send()
+
+        return carry
+
+    lax.fori_loop(0, NA, drain_a, 0)
+    lax.fori_loop(0, NB, drain_b, 0)
+    lax.fori_loop(0, NC, lambda j, c: (out_copy(j).wait(), c)[1], 0)
+    for k in range(4):
+        c_g(k).wait_send()
     for d in r17:
         c_rank(d).wait_send()
         c_hid(d).wait_send()
@@ -443,19 +605,23 @@
         kernel,
         out_shape=(
             jax.ShapeDtypeStruct((TOK, WIDTH), BF16),
-            jax.ShapeDtypeStruct((32, RANK, 256), F32),
+            jax.ShapeDtypeStruct((RANK, WIDTH), F32),
             jax.ShapeDtypeStruct((RANK, FEATS), F32),
             jax.ShapeDtypeStruct((KOUT, FEATS), F32),
         ),
-        in_specs=[hbm, hbm, hbm, vmem, vmem, vmem, hbm, vmem],
+        in_specs=[hbm, hbm, hbm, vmem, vmem, vmem, vmem, vmem],
         out_specs=(hbm, vmem, vmem, vmem),
         scratch_shapes=[
             pltpu.VMEM((TOK, WIDTH), BF16),
             pltpu.VMEM((8 * TOK, FEATS), BF16),
-            pltpu.VMEM((NC, PR, FEATS), jnp.int32),
-            pltpu.VMEM((WIDTH, RANK), BF16),
+            pltpu.VMEM((4 * TOK, FEATS), BF16),
+            pltpu.VMEM((4 * TOK, FEATS), BF16),
+            pltpu.VMEM((NA, PR, FEATS), jnp.int32),
+            pltpu.VMEM((PK, PR, FEATS), jnp.int32),
+            pltpu.VMEM((KOUT, 1), jnp.int32),
             pltpu.VMEM((RANK, WIDTH), BF16),
-            pltpu.VMEM((3, DC, FEATS), BF16),
+            pltpu.VMEM((NC, DC, FEATS), BF16),
+            pltpu.VMEM((NB, DC, FEATS), BF16),
             pltpu.VMEM((8, RANK, TOK), F32),
             pltpu.VMEM((8, RANK, TOK), F32),
             pltpu.VMEM((TOK, RANK), BF16),
@@ -466,26 +632,35 @@
             pltpu.VMEM((2, 4, 24, 384), F32),
             pltpu.VMEM((11, 24, 384), F32),
             pltpu.VMEM((2, 4, 24, 384), F32),
-            pltpu.VMEM((NC, 2, TOK, DC), BF16),
-            pltpu.VMEM((NC, 2, TOK, DC), BF16),
-            pltpu.VMEM((NC, 2, 2 * TOK, DC), BF16),
-            pltpu.VMEM((NC, 2, 2 * TOK, DC), BF16),
+            pltpu.VMEM((NA, 2, TOK, DC), BF16),
+            pltpu.VMEM((NA, 2, TOK, DC), BF16),
+            pltpu.VMEM((NA, 2, 2 * TOK, DC), BF16),
+            pltpu.VMEM((NA, 2, 2 * TOK, DC), BF16),
+            pltpu.VMEM((NA, TOK, DC), BF16),
+            pltpu.VMEM((NA, TOK, DC), BF16),
+            pltpu.VMEM((NA, TOK, DC), F32),
+            pltpu.VMEM((NB, 2, TOK // 2, DC), BF16),
+            pltpu.VMEM((NB, 2, TOK // 2, DC), BF16),
+            pltpu.VMEM((NB, 2, TOK, DC), BF16),
+            pltpu.VMEM((NB, 2, TOK, DC), BF16),
+            pltpu.VMEM((S2 + 1, 2 * TOK, DC), F32),
+            pltpu.VMEM((S3 + 1, TOK, DC), F32),
             pltpu.VMEM((NC, TOK, DC), BF16),
-            pltpu.VMEM((NC, TOK, DC), BF16),
-            pltpu.VMEM((NC, TOK, DC), F32),
-            pltpu.VMEM((NC, TOK, DC), BF16),
-            dma((3,)), dma((NC,)), dma((NC,)),
-            dma((NC, 2)), dma((NC, 2)), dma((NC, 2)), dma((NC, 2)),
-            dma((NC,)), dma((NC,)),
+            dma((2,)), dma((NA,)), dma((PK,)), dma((NC,)),
+            dma((NA, 2)), dma((NA, 2)), dma((NA, 2)), dma((NA, 2)),
+            dma((NA,)), dma((NA,)),
+            dma((NB, 2)), dma((NB, 2)), dma((NB, 2)), dma((NB, 2)),
+            dma((4,)), dma((4,)),
+            dma((NB,)), dma((NB,)), dma((NB,)), dma((NB, 3)), dma((NB, 3)), dma((NB,)), dma((NB,)),
             dma((8,)), dma((8,)), dma((8,)), dma((8,)),
             dma((21,)), dma((21,)), dma((11,)), dma((11,)),
         ],
         compiler_params=pltpu.CompilerParams(
-            collective_id=0, has_side_effects=True, vmem_limit_bytes=60 << 20
+            collective_id=0, has_side_effects=True, vmem_limit_bytes=62 << 20
         ),
         name="projection_backward",
-    )(act, g, pk, scale, idx.reshape(KOUT, 1), dfw, a, up)
-    return out, d.transpose(0, 2, 1).reshape(WIDTH, RANK), u, o
+    )(act, g, pk, scale, idx.reshape(1, KOUT), dfw, a.T, up)
+    return out, d.T, u, o
 
 
 def solution(mesh):

time: 181 us -> 143 us (0.79)
  Pallas kernels: 170 us -> 135 us
  local copies, waits for them, and re-layouts: 10.2 us -> 5.26 us
    pallas_call x1, Pallas kernels: 170 us -> 135 us  [body(): pl.pallas_call(kernel, out_shape=(jax.ShapeDtypeStruct((TOK, WIDTH), BF16...]
    reshape x2 -> x0, local copies, waits for them, and re-layouts: 3.23 us -> none  [the longest x1 1.87 us: body(): return (out, d.transpose(0, 2, 1).reshape(WIDTH, RANK), u, o)]
    unnamed x8 -> x10, local copies, waits for them, and re-layouts: 7.01 us -> 5.26 us
where the time goes in v2:
time: 143 us; the launch traced here: 141 us
  Pallas kernels  135 us (94%)
  local copies, waits for them, and re-layouts  5.26 us (4%)
    pallas_call x1, Pallas kernels, body(): pl.pallas_call(kernel, out_shape=(jax.ShapeDtypeStruct((TOK, WIDTH), BF16...  135 us
    unnamed x10, local copies, waits for them, and re-layouts  5.26 us

profile of v2, /device:TPU:16, one launch (start us, length us, event | category | flops | bytes accessed | tf_op | source)
XLA Modules:
  0.0 141.0 jit_solution(1745399673217825179)
XLA Ops:
  0.6 135.1 %projection_backward.1 = (bf16[128,8192]{1,0:T(8,128)(2,1)}, f32[16,8192]{1,0:T(8,128)}, f32[16,768]{1,0:T(8,128)}, f32[64,768]{1,0:T(8,128)}) custom-call(bf16[128,8192]{1,0:T(8,128)(2,1)} %act_h.1, bf16[1024,768]{1,0:T(8,128)(2,1)} %g_h.1, s32[2048,768]{1,0:T(8,128)} %pk_h.1, f32[64,768]{1,0:T(8,128)} %scale.1, s32[1,64]{1,0:T(1,128)} %bitcast.5, ...), custom_call_target="tpu_custom_call" | custom-call | tf_op jit(solution)/shard_map/projection_backward/pallas_call | solution.py:604
  135.7 0.0 copy-start
  135.8 0.0 copy-start.2
  135.8 0.0 copy-start.1
  135.8 3.2 %copy.16 = bf16[128,8192]{1,0:T(8,128)(2,1)} copy(bf16[128,8192]{1,0:T(8,128)(2,1)} %get-tuple-element.16) | data formatting | bytes 4194304
  138.9 0.0 copy-done
  138.9 0.8 copy.17
  139.7 0.0 copy-done.2
  139.7 0.6 copy.18
  140.4 0.0 copy-done.1
  140.4 0.7 copy.19
Async XLA Ops:
  135.7 3.2 %copy-start = (f32[16,8192]{1,0:T(8,128)S(1)}, f32[16,8192]{1,0:T(8,128)}, u32[]{:S(2)}) copy-start(f32[16,8192]{1,0:T(8,128)} %get-tuple-element.9) | copy-start | bytes 1572868
  135.8 4.0 %copy-start.2 = (f32[16,768]{1,0:T(8,128)S(1)}, f32[16,768]{1,0:T(8,128)}, u32[]{:S(2)}) copy-start(f32[16,768]{1,0:T(8,128)} %get-tuple-element.18) | copy-start | bytes 147460
  135.8 4.6 %copy-start.1 = (f32[64,768]{1,0:T(8,128)S(1)}, f32[64,768]{1,0:T(8,128)}, u32[]{:S(2)}) copy-start(f32[64,768]{1,0:T(8,128)} %get-tuple-element.19) | copy-start | bytes 589828

commit v3 on v2

--- a/solution.py
+++ b/solution.py
@@ -351,8 +351,6 @@
         for k in range(8):
             rank[k] = part_r[:, k * TOK:(k + 1) * TOK]
         rank_in[t] = rank[t]
-        for d in r17:
-            c_rank(d).start()
         cp_act.wait()
         total = jnp.zeros((HROWS, TOK), F32)
         step = 1024
@@ -364,8 +362,6 @@
             basis = jnp.concatenate([a_c, hot, zero], axis=0)
             total = total + mm(basis, act[:, cols], 1, 1)
         hid[t] = total.astype(BF16)
-        for d in r17:
-            c_hid(d).start()
 
     def arrange():
         shuf = unshuffle()
@@ -493,10 +489,13 @@
     unpack_a(0)
     cp_g.wait()
     stage1(0)
+    small0()
     pl.semaphore_wait(bar, len(peers))
     for i in range(2):
         c1(0, i).start()
-    small0()
+    for d in r17:
+        c_rank(d).start()
+        c_hid(d).start()
     for k in range(4):
         c_g(k).start()
 

time: 143 us -> 143 us (level)
  no operation moved by 1% of the time
where the time goes in v3:
time: 143 us; the launch traced here: 142 us
  Pallas kernels  136 us (95%)
  local copies, waits for them, and re-layouts  5.26 us (4%)
    pallas_call x1, Pallas kernels, body(): pl.pallas_call(kernel, out_shape=(jax.ShapeDtypeStruct((TOK, WIDTH), BF16...  136 us
    unnamed x10, local copies, waits for them, and re-layouts  5.26 us

profile of v3, /device:TPU:16, one launch (start us, length us, event | category | flops | bytes accessed | tf_op | source)
XLA Modules:
  0.0 142.2 jit_solution(11916396216794160948)
XLA Ops:
  0.6 136.2 %projection_backward.1 = (bf16[128,8192]{1,0:T(8,128)(2,1)}, f32[16,8192]{1,0:T(8,128)}, f32[16,768]{1,0:T(8,128)}, f32[64,768]{1,0:T(8,128)}) custom-call(bf16[128,8192]{1,0:T(8,128)(2,1)} %act_h.1, bf16[1024,768]{1,0:T(8,128)(2,1)} %g_h.1, s32[2048,768]{1,0:T(8,128)} %pk_h.1, f32[64,768]{1,0:T(8,128)} %scale.1, s32[1,64]{1,0:T(1,128)} %bitcast.5, ...), custom_call_target="tpu_custom_call" | custom-call | tf_op jit(solution)/shard_map/projection_backward/pallas_call | solution.py:603
  136.9 0.0 copy-start
  136.9 0.0 copy-start.2
  136.9 0.0 copy-start.1
  136.9 3.2 %copy.16 = bf16[128,8192]{1,0:T(8,128)(2,1)} copy(bf16[128,8192]{1,0:T(8,128)(2,1)} %get-tuple-element.16) | data formatting | bytes 4194304
  140.1 0.0 copy-done
  140.1 0.8 copy.17
  140.9 0.0 copy-done.2
  140.9 0.6 copy.18
  141.5 0.0 copy-done.1
  141.5 0.7 copy.19
Async XLA Ops:
  136.9 3.2 %copy-start = (f32[16,8192]{1,0:T(8,128)S(1)}, f32[16,8192]{1,0:T(8,128)}, u32[]{:S(2)}) copy-start(f32[16,8192]{1,0:T(8,128)} %get-tuple-element.9) | copy-start | bytes 1572868
  136.9 4.0 %copy-start.2 = (f32[16,768]{1,0:T(8,128)S(1)}, f32[16,768]{1,0:T(8,128)}, u32[]{:S(2)}) copy-start(f32[16,768]{1,0:T(8,128)} %get-tuple-element.18) | copy-start | bytes 147460
  136.9 4.6 %copy-start.1 = (f32[64,768]{1,0:T(8,128)S(1)}, f32[64,768]{1,0:T(8,128)}, u32[]{:S(2)}) copy-start(f32[64,768]{1,0:T(8,128)} %get-tuple-element.19) | copy-start | bytes 589828
